TPU v7x, 128 devices: a whole 4x4x4 slice. The times are simulated.
128 devices in a mesh: row: 16 (over x, z_lo, core), col: 8 (over z_hi, y).
Axes of the slice: x: 4, y: 4, z: 4 (z_hi: 2, z_lo: 2; z = z_hi * 2 + z_lo), core: 2. Of those that a mesh axis runs over, the one named last changes fastest.
Arguments:
- lambda_tiles: bfloat16 [96, 2048, 2048], P('row', 'col'), may hold values from -6 to 6
- dressing: bfloat16 [2048, 2048], P(('row', 'col')), may hold values from -0.125 to 0.125
- constant_term: bfloat16 [96, 2048, 2048], P('row', 'col'), may hold values from -6 to 6
- domain_mask: int32 [96, 32], P('row'), may hold values from 0 to 1, as said below
- virtual_energy: float32 [2048], replicated, may hold values from 0.2 to 1
- pair_shift: float32 [96], P('row'), may hold values from 0.1 to 1
Outputs:
- lambda_next: bfloat16 [96, 2048, 2048], P('row', 'col')
Inputs may be any that keep to these rules, and one draw needn't show every extreme that they name: `domain_mask`: each pair's domain is a nonempty subset of the 32 tiles; sizes differ from pair to pair.
All inputs are finite; a program needn't handle non-finite values.
Results may differ from a plain program's by a relative error of at most 0.001.
Values may be sent and summed in bfloat16 or wider, within the bound.
A program may use at most 128 MiB of HBM per device.

v0:
```python
import jax
import jax.numpy as jnp
from jax import lax
from jax.sharding import PartitionSpec as P

TILE = 64


def per_device(lambda_tiles, dressing, constant_term, domain_mask, virtual_energy, pair_shift):
    pair_count, row_count, full_width = lambda_tiles.shape
    col_start = lax.axis_index("col") * row_count
    tile_mask = jnp.repeat(domain_mask.astype(jnp.float32), TILE, axis=1)
    local_mask = lax.dynamic_slice_in_dim(tile_mask, col_start, row_count, 1)
    domain = local_mask[:, :, None] * tile_mask[:, None, :]
    masked = jnp.where(domain > 0, lambda_tiles, jnp.zeros_like(lambda_tiles))
    whole_dressing = lax.all_gather(dressing, ("row", "col"), axis=0, tiled=True)
    product = jnp.einsum("pae,eb->pab", masked, whole_dressing, preferred_element_type=jnp.float32)
    residual = domain * (constant_term.astype(jnp.float32) + product)
    squares = lax.psum(jnp.sum(residual * residual), ("row", "col"))
    entry_count = pair_count * lax.axis_size("row") * full_width * full_width
    factor = 0.25 * lax.rsqrt(squares / entry_count + 1e-06)
    energy_rows = lax.dynamic_slice_in_dim(virtual_energy, col_start, row_count, 0)
    denominator = (
        energy_rows[None, :, None] + virtual_energy[None, None, :] + pair_shift[:, None, None]
    )
    return (masked.astype(jnp.float32) + factor * residual / denominator).astype(jnp.bfloat16)


def solution(mesh):
    return jax.shard_map(
        per_device,
        mesh=mesh,
        in_specs=(
            P("row", "col", None),
            P(("row", "col"), None),
            P("row", "col", None),
            P("row", None),
            P(),
            P("row"),
        ),
        out_specs=P("row", "col", None),
        check_vma=False,
    )
```

profile of v0, /device:TPU:1, one launch (start us, length us, event | category | flops | bytes accessed | tf_op | source)
XLA Modules:
  0.0 431.3 jit_solution(2933205636144534346)
XLA Ops:
  6.5 0.0 all-gather.2.cloned.1.call-start
  6.5 0.7 all-gather.2.cloned.1.call-update
  7.3 0.7 convert_element_type.12
  8.0 0.1 broadcast_in_dim.4
  8.0 0.1 reshape.38
  8.1 0.8 dynamic_slice.7
  8.9 0.9 broadcast_add_fusion
  9.8 0.0 copy-start
  9.8 315.2 %all-gather.2.cloned.1.call-done = bf16[2048,2048]{1,0:T(8,128)(2,1)} async-done(((bf16[16,2048]{1,0:T(8,128)(2,1)}), bf16[2048,2048]{1,0:T(8,128)(2,1)}) %all-gather.2.cloned.1.call-update) | async-done | bytes 8388624 | tf_op jit(solution)/shard_map/all_gather | solution.py:16
  325.1 22.3 %multiply_reduce_fusion = (f32[]{:T(128)}, f32[6,256,2048]{2,1,0:T(8,128)}) fusion(bf16[2048,2048]{1,0:T(8,128)(2,1)} %all-gather.2.cloned.1.call-done, bf16[6,256,2048]{2,1,0:T(8,128)(2,1)} %param.6, f32[6,2048]{1,0:T(8,128)S(1)} %reshape.38, f32[6,256]{1,0:T(8,128)S(1)} %constant_dynamic-slice_fusion, bf16[6,256,2048]{2,1,0:T(8,128)(2,1)} %param.8), kind=kOutput, calls=%fused_computation.3 | convolution fusion | flops 12913213440 | bytes 33609732 | tf_op jit(solution)/shard_map/pae,eb->pab/dot_general | solution.py:17
  347.4 64.9 %psum.7 = f32[]{:T(128)} all-reduce(f32[]{:T(128)} %get-tuple-element.5), channel_id=1, replica_groups=mesh['row'=16,'col'=8] {'row','col'}, use_global_device_ids=true, to_apply=%region_1.2 | all-reduce | flops 1 | bytes 8 | tf_op jit(solution)/shard_map/psum | solution.py:19
  413.0 0.0 copy-done
  413.0 11.5 %add_convert_fusion = bf16[6,256,2048]{2,1,0:T(8,128)(2,1)} fusion(f32[6,256,2048]{2,1,0:T(8,128)} %get-tuple-element.6, f32[6]{0:T(128)S(1)} %copy-done, f32[256,2048]{1,0:T(8,128)S(1)} %broadcast_add_fusion, f32[]{:T(128)S(6)} %mul_shard_map.3, bf16[6,256,2048]{2,1,0:T(8,128)(2,1)} %param.6, f32[6,2048]{1,0:T(8,128)S(1)} %reshape.38, ...), kind=kLoop, calls=%fused_computation.2 | loop fusion | flops 28311552 | bytes 27318300 | tf_op jit(solution)/shard_map/convert_element_type | solution.py:26
  (1 shorter events, 0.0 us)
Async XLA Ops:
  6.5 318.5 %all-gather.2.cloned.1.call-start = ((), (), s32[]{:S(2)}) async-start(), calls=%async_computation | async-start | bytes 8454144 | tf_op jit(solution)/shard_map/all_gather | solution.py:16
  9.8 403.2 %copy-start = (f32[6]{0:T(128)S(1)}, f32[6]{0:T(128)}, u32[]{:S(2)}) copy-start(f32[6]{0:T(128)} %param.11) | copy-start | bytes 76
Sparse Core Ops, SparseCore 0:
  9.0 315.9 all-gather.1
where the time goes:
time: 432 us; the launch traced here: 431 us
  waiting for transfers between devices  316 us (73%)
  blocking collectives  64.9 us (15%)
  matrix products  22.3 us (5%)
  between operations  14.1 us (3%)
  other arithmetic  13.1 us (3%)
    all_gather x1, waiting for transfers between devices, per_device(): lax.all_gather(dressing, ('row', 'col'), axis=0, tiled=True)  315 us
    psum x1, blocking collectives, per_device(): squares = lax.psum(jnp.sum(residual * residual), ('row', 'col'))  64.9 us
    dot_general x1, matrix products, per_device(): jnp.einsum('pae,eb->pab', masked, whole_dressing, preferred_element_type=...  22.3 us
    convert_element_type x1, other arithmetic, per_device(): (masked.astype(jnp.float32) + factor * residual / denominator).astype(jnp...  11.5 us
  transfers between devices with their start and end apart: 1, of which 1 were waited for; matrix products, arithmetic and copies ran while one was open for 1% of the time, Pallas kernels for 0%

commit v1 on v0

v1 whole, which is shorter than its diff:
```python
import jax
import jax.numpy as jnp
from jax import lax
from jax.experimental import pallas as pl
from jax.experimental.pallas import tpu as pltpu
from jax.sharding import PartitionSpec as P

MESH = pl.DeviceIdType.MESH
F32, BF16 = jnp.float32, jnp.bfloat16
TILE = 64
PAIRS, ROWS, V = 6, 256, 2048
WIDTH = 256
STRIPS = V // WIDTH
DEVICES = 128
ENTRIES = 96 * V * V
ORDERS = ("yzx", "xyz", "zxy")
HOPS = (2, 1, 3)
MTILE = 768


def place():
    row, col = lax.axis_index("row"), lax.axis_index("col")
    return {
        "x": row // 4,
        "zl": (row // 2) % 2,
        "c": row % 2,
        "zh": col // 4,
        "y": col % 4,
        "z": (col // 4) * 2 + (row // 2) % 2,
    }


def device(at):
    return {"row": at["x"] * 4 + (at["z"] % 2) * 2 + at["c"], "col": (at["z"] // 2) * 4 + at["y"]}


def neighbour(at, axis, hops):
    moved = dict(at)
    moved[axis] = (at[axis] + hops) % 4
    return device(moved)


def sibling(at):
    moved = dict(at)
    moved["c"] = 1 - at["c"]
    return device(moved)


def block(gathered, strip, at, whole):
    every = slice(None)
    return gathered.at[
        strip,
        every if "x" in whole else at["x"],
        every if "z" in whole else at["zl"],
        at["c"],
        every if "z" in whole else at["zh"],
        every if "y" in whole else at["y"],
    ]


def gather_kernel(
    lam_hbm, dress_hbm, const_hbm, mask_ref, energy_ref, shift_ref,
    resid_ref, masked_ref, factor_ref,
    gathered, const_ref, colmask, rowmask, squares, mine, everyone,
    load_sem, own_sem, send_sem, recv_sem, sib_send, sib_recv, sum_send, sum_recv,
):
    at = place()
    barrier = pltpu.get_barrier_semaphore()
    partners = [neighbour(at, axis, hops) for axis in "xyz" for hops in HOPS] + [sibling(at)]
    for partner in partners:
        pl.semaphore_signal(barrier, inc=1, device_id=partner, device_id_type=MESH)

    own = [
        pltpu.make_async_copy(
            dress_hbm.at[:, pl.ds(s * WIDTH, WIDTH)], block(gathered, s, at, ""), own_sem.at[s]
        )
        for s in range(STRIPS)
    ]
    for copy in own:
        copy.start()
    loads = []
    for p in range(PAIRS):
        rows = pl.ds(p * ROWS, ROWS)
        loads.append(pltpu.make_async_copy(lam_hbm.at[p], masked_ref.at[rows, :], load_sem.at[0, p]))
        loads.append(pltpu.make_async_copy(const_hbm.at[p], const_ref.at[rows, :], load_sem.at[1, p]))
    for copy in loads:
        copy.start()
    for copy in own:
        copy.wait()
    pl.semaphore_wait(barrier, len(partners))

    def spread(phase, s):
        order = ORDERS[s % 3]
        part = block(gathered, s, at, order[:phase])
        return [
            pltpu.make_async_remote_copy(
                src_ref=part,
                dst_ref=part,
                send_sem=send_sem.at[phase, s, k],
                recv_sem=recv_sem.at[phase, s, k],
                device_id=neighbour(at, order[phase], hops),
                device_id_type=MESH,
            )
            for k, hops in enumerate(HOPS)
        ]

    sent = []

    def start(copies):
        for copy in copies:
            copy.start()
        sent.extend(copies)
        return copies

    first = [start(spread(0, s)) for s in range(STRIPS)]

    mask = mask_ref[...].astype(F32)
    tile_of = lax.broadcasted_iota(jnp.int32, (VT, V), 0)
    tile_col = lax.broadcasted_iota(jnp.int32, (VT, V), 1) // TILE
    cols_of = jnp.dot(mask, (tile_of == tile_col).astype(F32), preferred_element_type=F32)
    col = lax.axis_index("col")
    row_tile = lax.broadcasted_iota(jnp.int32, (ROWS, VT), 0) // TILE + col * (ROWS // TILE)
    row_hot = (row_tile == lax.broadcasted_iota(jnp.int32, (ROWS, VT), 1)).astype(F32)
    for p in range(PAIRS):
        colmask[p] = cols_of[p : p + 1, :]
        rowmask[p] = jnp.sum(row_hot * mask[p : p + 1, :], axis=1, keepdims=True)

    def prepare(pairs):
        for p in pairs:
            rows = pl.ds(p * ROWS, ROWS)
            loads[2 * p].wait()
            loads[2 * p + 1].wait()
            domain = (rowmask[p] * colmask[p]).astype(BF16)
            masked_ref[rows, :] = masked_ref[rows, :] * domain
            const_ref[rows, :] = const_ref[rows, :] * domain

    second, third = [], []
    for s in range(STRIPS):
        for copy in first[s]:
            copy.wait_recv()
        second.append(start(spread(1, s)))
    prepare(range(PAIRS))
    for s in range(STRIPS):
        for copy in second[s]:
            copy.wait_recv()
        third.append(start(spread(2, s)))

    def hand_over(s):
        part = block(gathered, s, at, "xyz")
        return pltpu.make_async_remote_copy(
            src_ref=part,
            dst_ref=part,
            send_sem=sib_send.at[s],
            recv_sem=sib_recv.at[s],
            device_id=sibling(at),
            device_id_type=MESH,
        )

    across = []

    def land(s):
        for copy in third[s]:
            copy.wait_recv()
        across.append(hand_over(s))
        across[s].start()

    squares[...] = jnp.zeros_like(squares)

    def multiply(s):
        cols = pl.ds(s * WIDTH, WIDTH)

        def tile(i, carry):
            rows = pl.ds(pl.multiple_of(i * MTILE, MTILE), MTILE)
            strip = gathered[s].reshape(V, WIDTH)
            product = jnp.dot(masked_ref[rows, :], strip, preferred_element_type=F32)
            total = jnp.zeros((8, WIDTH), F32)
            for q in range(MTILE // ROWS):
                pair_rows = pl.ds(pl.multiple_of(i * MTILE + q * ROWS, ROWS), ROWS)
                inside = colmask[i * (MTILE // ROWS) + q, :, cols]
                part = const_ref[pair_rows, cols].astype(F32) + inside * product[q * ROWS : (q + 1) * ROWS, :]
                resid_ref[pair_rows, cols] = part
                total = total + jnp.sum((part * part).reshape(ROWS // 8, 8, WIDTH), axis=0)
            squares[...] += total
            return carry

        lax.fori_loop(0, PAIRS * ROWS // MTILE, tile, 0)

    land(0)
    for s in range(STRIPS):
        if s + 1 < STRIPS:
            land(s + 1)
        across[s].wait_recv()
        multiply(s)

    eight = squares[:, :128] + squares[:, 128:]
    mine[...] = jnp.sum(eight, axis=0, keepdims=True)
    me = lax.axis_index("row") * 8 + col
    sums = []
    for step in range(1, DEVICES):
        other = (me + step) % DEVICES
        sums.append(
            pltpu.make_async_remote_copy(
                src_ref=mine,
                dst_ref=everyone.at[me],
                send_sem=sum_send.at[step],
                recv_sem=sum_recv.at[step],
                device_id={"row": other // 8, "col": other % 8},
                device_id_type=MESH,
            )
        )
    for copy in sums:
        copy.start()
    everyone[me] = mine[...]

    start_col = pl.multiple_of(col * ROWS, ROWS)
    own_energy = energy_ref[:, pl.ds(start_col, ROWS)]
    diagonal = lax.broadcasted_iota(jnp.int32, (ROWS, ROWS), 0) == lax.broadcasted_iota(jnp.int32, (ROWS, ROWS), 1)
    energy_rows = jnp.sum(jnp.where(diagonal, own_energy, 0.0), axis=1, keepdims=True)

    for p in range(PAIRS):
        shifted = energy_rows + shift_ref[p]
        for s in range(STRIPS):
            rows, cols = pl.ds(p * ROWS, ROWS), pl.ds(s * WIDTH, WIDTH)
            resid_ref[rows, cols] = resid_ref[rows, cols] / (shifted + energy_ref[:, cols])

    for copy in sums:
        copy.wait_recv()
    total = jnp.sum(jnp.sum(everyone[...], axis=0), axis=1, keepdims=True)
    factor = 0.25 * lax.rsqrt(total / ENTRIES + 1e-06)
    factor_ref[...] = jnp.zeros((8, 128), F32) + factor

    for copy in sent + across + sums:
        copy.wait_send()


VT = V // TILE
CHUNK = 128


def update_kernel(resid_ref, masked_ref, factor_ref, out_hbm, staged, sem):
    factor = factor_ref[0:1, 0:1]
    copies = []
    for i in range(PAIRS * ROWS // CHUNK):
        rows = pl.ds(i * CHUNK, CHUNK)
        staged[rows, :] = (masked_ref[rows, :].astype(F32) + factor * resid_ref[rows, :]).astype(BF16)
        copies.append(pltpu.make_async_copy(staged.at[rows, :], out_hbm.at[rows, :], sem.at[i]))
        copies[-1].start()
    for copy in copies:
        copy.wait()


def per_device(lambda_tiles, dressing, constant_term, domain_mask, virtual_energy, pair_shift):
    vmem, hbm, smem = (pl.BlockSpec(memory_space=m) for m in (pltpu.VMEM, pl.ANY, pltpu.SMEM))
    flat = (PAIRS * ROWS, V)
    dma = pltpu.SemaphoreType.DMA
    resid, masked, factor = pl.pallas_call(
        gather_kernel,
        name="gather_multiply",
        out_shape=(pltpu.VMEM(flat, F32), pltpu.VMEM(flat, BF16), pltpu.VMEM((8, 128), F32)),
        in_specs=[hbm, hbm, hbm, vmem, vmem, smem],
        out_specs=(vmem, vmem, vmem),
        scratch_shapes=[
            pltpu.VMEM((STRIPS, 4, 2, 2, 2, 4, 16, WIDTH), BF16),
            pltpu.VMEM(flat, BF16),
            pltpu.VMEM((PAIRS, 1, V), F32),
            pltpu.VMEM((PAIRS, ROWS, 1), F32),
            pltpu.VMEM((8, WIDTH), F32),
            pltpu.VMEM((1, 128), F32),
            pltpu.VMEM((DEVICES, 1, 128), F32),
            dma((2, PAIRS)),
            dma((STRIPS,)),
            dma((3, STRIPS, 3)),
            dma((3, STRIPS, 3)),
            dma((STRIPS,)),
            dma((STRIPS,)),
            dma((DEVICES,)),
            dma((DEVICES,)),
        ],
        compiler_params=pltpu.CompilerParams(
            collective_id=0, has_side_effects=True, vmem_limit_bytes=36 << 20
        ),
    )(lambda_tiles, dressing, constant_term, domain_mask, virtual_energy.reshape(1, V), pair_shift)
    resid = pltpu.with_memory_space_constraint(resid, pltpu.VMEM)
    masked = pltpu.with_memory_space_constraint(masked, pltpu.VMEM)
    out = pl.pallas_call(
        update_kernel,
        name="scale_update",
        out_shape=jax.ShapeDtypeStruct(flat, BF16),
        in_specs=[vmem, vmem, vmem],
        out_specs=hbm,
        scratch_shapes=[pltpu.VMEM(flat, BF16), dma((PAIRS * ROWS // CHUNK,))],
        compiler_params=pltpu.CompilerParams(vmem_limit_bytes=16 << 20),
    )(resid, masked, factor)
    return out.reshape(PAIRS, ROWS, V)


def solution(mesh):
    return jax.shard_map(
        per_device,
        mesh=mesh,
        in_specs=(
            P("row", "col", None),
            P(("row", "col"), None),
            P("row", "col", None),
            P("row", None),
            P(),
            P("row"),
        ),
        out_specs=P("row", "col", None),
        check_vma=False,
    )
```

time: 432 us -> 60 us (0.14)
  waiting for transfers between devices: 316 us -> 0 us
  blocking collectives: 64.9 us -> 0 us
  Pallas kernels: 0 us -> 59.7 us
  matrix products: 22.3 us -> 0 us
  between operations: 14.1 us -> 0.17 us
  other arithmetic: 13.1 us -> 0 us
    all_gather x1 -> x0, waiting for transfers between devices: 315 us -> none  [per_device(): lax.all_gather(dressing, ('row', 'col'), axis=0, tiled=True)]
    psum x1 -> x0, blocking collectives: 64.9 us -> none  [per_device(): squares = lax.psum(jnp.sum(residual * residual), ('row', 'col'))]
    pallas_call x0 -> x2, Pallas kernels: none -> 59.7 us  [the longest x1 56 us: per_device(): pl.pallas_call(gather_kernel, name='gather_multiply', out_shape=(pltpu.VM...]
    dot_general x1 -> x0, matrix products: 22.3 us -> none  [per_device(): jnp.einsum('pae,eb->pab', masked, whole_dressing, preferred_element_type=...]
    convert_element_type x2 -> x0, other arithmetic: 12.2 us -> none  [the longest x1 11.5 us: per_device(): (masked.astype(jnp.float32) + factor * residual / denominator).astype(jnp...]
  transfers between devices with their start and end apart: 1 -> 0, of which waited for: 1 -> 0; matrix products, arithmetic and copies ran while one was open for 1% -> 0% of each run, Pallas kernels for 0% -> 0%
where the time goes in v1:
time: 60 us; the launch traced here: 59.8 us
  Pallas kernels  59.7 us (100%)
    pallas_call x1, Pallas kernels, per_device(): pl.pallas_call(gather_kernel, name='gather_multiply', out_shape=(pltpu.VM...  56 us
    pallas_call x1, Pallas kernels, per_device(): pl.pallas_call(update_kernel, name='scale_update', out_shape=jax.ShapeDty...  3.66 us

profile of v1, /device:TPU:1, one launch (start us, length us, event | category | flops | bytes accessed | tf_op | source)
XLA Modules:
  0.0 59.8 jit_solution(9187023850714497353)
XLA Ops:
  0.0 56.0 %gather_multiply.1 = (f32[1536,2048]{1,0:T(8,128)S(1)}, bf16[1536,2048]{1,0:T(8,128)(2,1)S(1)}, f32[8,128]{1,0:T(8,128)S(1)}) custom-call(bf16[6,256,2048]{2,1,0:T(8,128)(2,1)} %lam_hbm.1, bf16[16,2048]{1,0:T(8,128)(2,1)} %dress_hbm.1, bf16[6,256,2048]{2,1,0:T(8,128)(2,1)} %const_hbm.1, s32[6,32]{1,0:T(8,128)} %mask_ref.1, f32[1,2048]{1,0:T(1,128)} %bitcast.2, ...), custom_call_target="tpu_custom_call" | custom-call | tf_op jit(solution)/shard_map/gather_multiply/pallas_call | solution.py:256
  56.0 3.7 %scale_update.1 = bf16[1536,2048]{1,0:T(8,128)(2,1)} custom-call(f32[1536,2048]{1,0:T(8,128)S(1)} %get-tuple-element.8.resid_ref, bf16[1536,2048]{1,0:T(8,128)(2,1)S(1)} %get-tuple-element.9.masked_ref, f32[8,128]{1,0:T(8,128)S(1)} %get-tuple-element.10.factor_ref), custom_call_target="tpu_custom_call" | custom-call | tf_op jit(solution)/shard_map/scale_update/pallas_call | solution.py:285

commit v2 on v1

v2 whole, which is shorter than its diff:
```python
import jax
import jax.numpy as jnp
from jax import lax
from jax.experimental import pallas as pl
from jax.experimental.pallas import tpu as pltpu
from jax.sharding import PartitionSpec as P

MESH = pl.DeviceIdType.MESH
F32, BF16 = jnp.float32, jnp.bfloat16
TILE = 64
PAIRS, ROWS, V = 6, 256, 2048
WIDTH = 256
STRIPS = V // WIDTH
DEVICES = 128
ENTRIES = 96 * V * V
ORDERS = ("yzx", "xyz", "zxy")
VT = V // TILE
GROUPS = ((0, 1, 2), (3, 4, 5), (6, 7))
STREAMS = ("one", "two", "ring", "relay", "side")


def place():
    row, col = lax.axis_index("row"), lax.axis_index("col")
    return {
        "x": row // 4,
        "zl": (row // 2) % 2,
        "c": row % 2,
        "zh": col // 4,
        "y": col % 4,
        "z": (col // 4) * 2 + (row // 2) % 2,
    }


def device(at):
    return {"row": at["x"] * 4 + (at["z"] % 2) * 2 + at["c"], "col": (at["z"] // 2) * 4 + at["y"]}


def neighbour(at, axis, hops):
    moved = dict(at)
    moved[axis] = (at[axis] + hops) % 4
    return device(moved)


def sibling(at):
    moved = dict(at)
    moved["c"] = 1 - at["c"]
    return device(moved)


def block(gathered, strip, at, whole, half=None):
    every = slice(None)
    x, zl = (every if "x" in whole else at["x"]), (every if "z" in whole else at["zl"])
    if half is not None:
        if "x" in whole:
            x = pl.ds(2 * half, 2)
        else:
            zl = half
    return gathered.at[
        strip,
        x,
        zl,
        every if "z" in whole else at["zh"],
        at["c"],
        every if "y" in whole else at["y"],
    ]


def moved(at, axis, hops):
    there = dict(at)
    there[axis] = (at[axis] + hops) % 4
    if axis == "z":
        there["zl"], there["zh"] = there["z"] % 2, there["z"] // 2
    return there


def gather_kernel(
    lam_hbm, dress_hbm, const_hbm, mask_hbm, energy_hbm, shift_hbm,
    resid_ref, masked_ref, factor_ref,
    gathered, turned, const_ref, mask_ref, energy_ref, shift_ref, colmask, rowmask, squares, mine, everyone,
    small_sem, load_sem, own_sem, send_sem, recv_one, recv_two, recv_ring, recv_relay, recv_side, sum_send, sum_recv,
):
    at = place()
    col = lax.axis_index("col")
    other_core = dict(at, c=1 - at["c"])
    barrier = pltpu.get_barrier_semaphore()
    partners = [device(moved(at, axis, hops)) for axis in "xyz" for hops in (2, 1, 3)] + [device(other_core)]
    for partner in partners:
        pl.semaphore_signal(barrier, inc=1, device_id=partner, device_id_type=MESH)

    own = [
        pltpu.make_async_copy(dress_hbm.at[:, pl.ds(s * WIDTH, WIDTH)], block(gathered, s, at, ""), own_sem)
        for s in range(STRIPS)
    ]
    for copy in own:
        copy.start()
    small = [
        pltpu.make_async_copy(mask_hbm, mask_ref, small_sem.at[0]),
        pltpu.make_async_copy(energy_hbm, energy_ref, small_sem.at[1]),
        pltpu.make_async_copy(shift_hbm, shift_ref, small_sem.at[2]),
    ]
    for copy in small:
        copy.start()
    loads = []
    for p in range(PAIRS):
        rows = pl.ds(p * ROWS, ROWS)
        loads.append(pltpu.make_async_copy(lam_hbm.at[p], masked_ref.at[rows, :], load_sem.at[0, p]))
        loads.append(pltpu.make_async_copy(const_hbm.at[p], const_ref.at[rows, :], load_sem.at[1, p]))
    for copy in loads:
        copy.start()

    def wait_blocks(ref, sem):
        pltpu.make_async_copy(ref, ref, sem).wait()

    wait_blocks(gathered.at[:, 0, 0, 0, 0, 0], own_sem)
    pl.semaphore_wait(barrier, len(partners))

    def send(part, target, stream, recv):
        pltpu.make_async_remote_copy(
            src_ref=part,
            dst_ref=part,
            send_sem=send_sem.at[STREAMS.index(stream)],
            recv_sem=recv,
            device_id=device(target),
            device_id_type=MESH,
        ).start()

    def spread_one(s):
        order = ORDERS[s % 3]
        for hops in (2, 1, 3):
            send(block(gathered, s, at, ""), moved(at, order[0], hops), "one", recv_one)

    def spread_two(s):
        order = ORDERS[s % 3]
        for hops in (2, 1, 3):
            send(block(gathered, s, at, order[0]), moved(at, order[1], hops), "two", recv_two.at[s])

    def spread_ring(s):
        order = ORDERS[s % 3]
        for hops in (1, 3):
            send(block(gathered, s, at, order[:2]), moved(at, order[2], hops), "ring", recv_ring.at[s])
        send(block(gathered, s, at, order[:2]), other_core, "side", recv_side.at[0, s])

    def relay(s):
        order = ORDERS[s % 3]
        wait_blocks(gathered.at[s, 0:2, :, :, 0, :], recv_ring.at[s])
        for hops, half in ((1, 0), (3, 1)):
            source = moved(at, order[2], -hops)
            send(block(gathered, s, source, order[:2], half), moved(at, order[2], hops), "relay", recv_relay.at[s])
        for hops in (1, 3):
            send(block(gathered, s, moved(at, order[2], hops), order[:2]), other_core, "side", recv_side.at[1, s])

    def land(s):
        order = ORDERS[s % 3]
        wait_blocks(gathered.at[s, 0, :, :, 0, :], recv_relay.at[s])
        send(block(gathered, s, moved(at, order[2], 2), order[:2]), other_core, "side", recv_side.at[2, s])

    def ready(s):
        wait_blocks(gathered.at[s, 0, :, :, 0, :], recv_side.at[0, s])
        wait_blocks(gathered.at[s, 0:2, :, :, 0, :], recv_side.at[1, s])
        wait_blocks(gathered.at[s, 0, :, :, 0, :], recv_side.at[2, s])

    for s in range(STRIPS):
        spread_one(s)

    for copy in small:
        copy.wait()
    mask = mask_ref[...].astype(F32)
    tile_of = lax.broadcasted_iota(jnp.int32, (VT, V), 0)
    tile_col = lax.broadcasted_iota(jnp.int32, (VT, V), 1) // TILE
    cols_of = jnp.dot(mask, (tile_of == tile_col).astype(F32), preferred_element_type=F32)
    row_tile = lax.broadcasted_iota(jnp.int32, (ROWS, VT), 0) // TILE + col * (ROWS // TILE)
    row_hot = (row_tile == lax.broadcasted_iota(jnp.int32, (ROWS, VT), 1)).astype(F32)
    for p in range(PAIRS):
        colmask[p] = cols_of[p : p + 1, :]
        rowmask[p] = jnp.sum(row_hot * mask[p : p + 1, :], axis=1, keepdims=True)
    squares[...] = jnp.zeros_like(squares)

    wait_blocks(gathered.at[:, 0:3, 0, 0, 0, 0], recv_one)
    for s in range(STRIPS):
        spread_two(s)

    def prepare(p):
        rows = pl.ds(p * ROWS, ROWS)
        loads[2 * p].wait()
        loads[2 * p + 1].wait()
        for q in range(V // 256):
            cols = pl.ds(q * 256, 256)
            domain = (rowmask[p] * colmask[p, :, cols]).astype(BF16)
            part = masked_ref[rows, cols] * domain
            masked_ref[rows, cols] = part
            pieces = [part[:, k * 64 : (k + 1) * 64] for k in (0, 2, 1, 3)]
            turned[rows, cols] = jnp.concatenate(pieces, axis=1)
            const_ref[rows, cols] = const_ref[rows, cols] * domain

    def arrive_two(s):
        wait_blocks(gathered.at[s, 0:3, 0, 0, 0, :], recv_two.at[s])
        spread_ring(s)

    for p in (0, 1, 2):
        prepare(p)
    for s in GROUPS[0]:
        arrive_two(s)
    for p in (3, 4, 5):
        prepare(p)
    for s in GROUPS[1]:
        arrive_two(s)

    def multiply(first, last):
        def strip(s, carry):
            cols = pl.ds(pl.multiple_of(s * WIDTH, WIDTH), WIDTH)
            right = gathered[s].reshape(V, WIDTH)
            product = jnp.dot(turned[...], right, preferred_element_type=F32)
            total = jnp.zeros((8, WIDTH), F32)
            for p in range(PAIRS):
                rows = pl.ds(p * ROWS, ROWS)
                part = const_ref[rows, cols].astype(F32) + colmask[p, :, cols] * product[p * ROWS : (p + 1) * ROWS, :]
                resid_ref[rows, cols] = part
                total = total + jnp.sum((part * part).reshape(ROWS // 8, 8, WIDTH), axis=0)
            squares[...] += total
            return carry

        lax.fori_loop(first, last, strip, 0)

    for s in GROUPS[0]:
        relay(s)
    for s in GROUPS[2]:
        arrive_two(s)
    for s in GROUPS[1]:
        relay(s)
    for s in GROUPS[0]:
        land(s)
    for s in GROUPS[0]:
        ready(s)
    multiply(0, 2)
    for s in GROUPS[2]:
        relay(s)
    for s in GROUPS[1]:
        land(s)
    multiply(2, 3)
    for s in GROUPS[1]:
        ready(s)
    multiply(3, 5)
    for s in GROUPS[2]:
        land(s)
    multiply(5, 6)
    for s in GROUPS[2]:
        ready(s)
    multiply(6, 8)

    eight = squares[:, :128] + squares[:, 128:]
    mine[...] = jnp.sum(eight, axis=0, keepdims=True)
    me = lax.axis_index("row") * 8 + col

    def tell(step, carry):
        other = (me + step) % DEVICES
        pltpu.make_async_remote_copy(
            src_ref=mine,
            dst_ref=everyone.at[me],
            send_sem=sum_send,
            recv_sem=sum_recv,
            device_id={"row": other // 8, "col": other % 8},
            device_id_type=MESH,
        ).start()
        return carry

    lax.fori_loop(1, DEVICES, tell, 0, unroll=True)
    everyone[me] = mine[...]

    own_energy = energy_ref[:, pl.ds(pl.multiple_of(col * ROWS, ROWS), ROWS)]
    diagonal = lax.broadcasted_iota(jnp.int32, (ROWS, ROWS), 0) == lax.broadcasted_iota(jnp.int32, (ROWS, ROWS), 1)
    energy_rows = jnp.sum(jnp.where(diagonal, own_energy, 0.0), axis=1, keepdims=True)

    def divide(p, carry):
        shifted = energy_rows + shift_ref[p]
        for s in range(STRIPS):
            rows, cols = pl.ds(pl.multiple_of(p * ROWS, ROWS), ROWS), pl.ds(s * WIDTH, WIDTH)
            resid_ref[rows, cols] = resid_ref[rows, cols] / (shifted + energy_ref[:, cols])
        return carry

    lax.fori_loop(0, PAIRS, divide, 0)

    wait_blocks(everyone.at[0 : DEVICES - 1], sum_recv)
    total = jnp.sum(jnp.sum(everyone[...], axis=0), axis=1, keepdims=True)
    factor = 0.25 * lax.rsqrt(total / ENTRIES + 1e-06)
    factor_ref[...] = jnp.zeros((8, 128), F32) + factor

    wait_blocks(gathered.at[:, 0:3, 0, 0, 0, 0], send_sem.at[0])
    wait_blocks(gathered.at[:, 0:3, 0, 0, 0, :], send_sem.at[1])
    wait_blocks(gathered.at[:, :, :, :, 0, 0:2], send_sem.at[2])
    wait_blocks(gathered.at[:, :, :, :, 0, 0], send_sem.at[3])
    wait_blocks(gathered.at[:, :, :, :, 0, :], send_sem.at[4])
    wait_blocks(everyone.at[0 : DEVICES - 1], sum_send)


CHUNK = 128


def update_kernel(resid_ref, masked_ref, factor_ref, out_hbm, staged, sem):
    factor = factor_ref[0:1, 0:1]
    copies = []
    for i in range(PAIRS * ROWS // CHUNK):
        rows = pl.ds(i * CHUNK, CHUNK)
        staged[rows, :] = (masked_ref[rows, :].astype(F32) + factor * resid_ref[rows, :]).astype(BF16)
        copies.append(pltpu.make_async_copy(staged.at[rows, :], out_hbm.at[rows, :], sem.at[i]))
        copies[-1].start()
    for copy in copies:
        copy.wait()


def per_device(lambda_tiles, dressing, constant_term, domain_mask, virtual_energy, pair_shift):
    vmem, hbm = (pl.BlockSpec(memory_space=m) for m in (pltpu.VMEM, pl.ANY))
    flat = (PAIRS * ROWS, V)
    dma = pltpu.SemaphoreType.DMA
    resid, masked, factor = pl.pallas_call(
        gather_kernel,
        name="gather_multiply",
        out_shape=(pltpu.VMEM(flat, F32), pltpu.VMEM(flat, BF16), pltpu.VMEM((8, 128), F32)),
        in_specs=[hbm] * 6,
        out_specs=(vmem, vmem, vmem),
        scratch_shapes=[
            pltpu.VMEM((STRIPS, 4, 2, 2, 2, 4, 16, WIDTH), BF16),
            pltpu.VMEM(flat, BF16),
            pltpu.VMEM(flat, BF16),
            pltpu.VMEM((PAIRS, VT), jnp.int32),
            pltpu.VMEM((1, V), F32),
            pltpu.SMEM((PAIRS,), F32),
            pltpu.VMEM((PAIRS, 1, V), F32),
            pltpu.VMEM((PAIRS, ROWS, 1), F32),
            pltpu.VMEM((8, WIDTH), F32),
            pltpu.VMEM((1, 128), F32),
            pltpu.VMEM((DEVICES, 1, 128), F32),
            dma((3,)),
            dma((2, PAIRS)),
            dma,
            dma((len(STREAMS),)),
            dma,
            dma((STRIPS,)),
            dma((STRIPS,)),
            dma((STRIPS,)),
            dma((3, STRIPS)),
            dma,
            dma,
        ],
        compiler_params=pltpu.CompilerParams(
            collective_id=0, has_side_effects=True, vmem_limit_bytes=36 << 20
        ),
    )(lambda_tiles, dressing, constant_term, domain_mask, virtual_energy.reshape(1, V), pair_shift)
    resid = pltpu.with_memory_space_constraint(resid, pltpu.VMEM)
    masked = pltpu.with_memory_space_constraint(masked, pltpu.VMEM)
    out = pl.pallas_call(
        update_kernel,
        name="scale_update",
        out_shape=jax.ShapeDtypeStruct(flat, BF16),
        in_specs=[vmem, vmem, vmem],
        out_specs=hbm,
        scratch_shapes=[pltpu.VMEM(flat, BF16), dma((PAIRS * ROWS // CHUNK,))],
        compiler_params=pltpu.CompilerParams(vmem_limit_bytes=16 << 20),
    )(resid, masked, factor)
    return out.reshape(PAIRS, ROWS, V)


def solution(mesh):
    return jax.shard_map(
        per_device,
        mesh=mesh,
        in_specs=(
            P("row", "col", None),
            P(("row", "col"), None),
            P("row", "col", None),
            P("row", None),
            P(),
            P("row"),
        ),
        out_specs=P("row", "col", None),
        check_vma=False,
    )
```

time: 60 us -> 56.7 us (0.945)
  Pallas kernels: 59.7 us -> 56.4 us
    pallas_call x1, Pallas kernels: 56 us -> 52.7 us  [per_device(): pl.pallas_call(gather_kernel, name='gather_multiply', out_shape=(pltpu.VM...]
where the time goes in v2:
time: 56.7 us; the launch traced here: 56.6 us
  Pallas kernels  56.4 us (99%)
    pallas_call x1, Pallas kernels, per_device(): pl.pallas_call(gather_kernel, name='gather_multiply', out_shape=(pltpu.VM...  52.7 us
    pallas_call x1, Pallas kernels, per_device(): pl.pallas_call(update_kernel, name='scale_update', out_shape=jax.ShapeDty...  3.66 us

profile of v2, /device:TPU:1, one launch (start us, length us, event | category | flops | bytes accessed | tf_op | source)
XLA Modules:
  0.0 56.6 jit_solution(3820951028660044767)
XLA Ops:
  0.0 52.7 %gather_multiply.1 = (f32[1536,2048]{1,0:T(8,128)S(1)}, bf16[1536,2048]{1,0:T(8,128)(2,1)S(1)}, f32[8,128]{1,0:T(8,128)S(1)}) custom-call(bf16[6,256,2048]{2,1,0:T(8,128)(2,1)} %lam_hbm.1, bf16[16,2048]{1,0:T(8,128)(2,1)} %dress_hbm.1, bf16[6,256,2048]{2,1,0:T(8,128)(2,1)} %const_hbm.1, s32[6,32]{1,0:T(8,128)} %mask_hbm.1, f32[1,2048]{1,0:T(1,128)} %bitcast.2, ...), custom_call_target="tpu_custom_call" | custom-call | tf_op jit(solution)/shard_map/gather_multiply/pallas_call | solution.py:314
  52.7 3.7 %scale_update.1 = bf16[1536,2048]{1,0:T(8,128)(2,1)} custom-call(f32[1536,2048]{1,0:T(8,128)S(1)} %get-tuple-element.8.resid_ref, bf16[1536,2048]{1,0:T(8,128)(2,1)S(1)} %get-tuple-element.9.masked_ref, f32[8,128]{1,0:T(8,128)S(1)} %get-tuple-element.10.factor_ref), custom_call_target="tpu_custom_call" | custom-call | tf_op jit(solution)/shard_map/scale_update/pallas_call | solution.py:350

commit v3 on v2

--- a/solution.py
+++ b/solution.py
@@ -13,9 +13,11 @@
 STRIPS = V // WIDTH
 DEVICES = 128
 ENTRIES = 96 * V * V
-ORDERS = ("yzx", "xyz", "zxy")
+ORDERS = ("yzx", "xyz", "zxy", "yzx", "xyz", "zxy", "yzx", "xyz")
 VT = V // TILE
 GROUPS = ((0, 1, 2), (3, 4, 5), (6, 7))
+MTILE = 1536
+AHEAD = 2
 STREAMS = ("one", "two", "ring", "relay", "side")
 
 
@@ -33,18 +35,6 @@
 
 def device(at):
     return {"row": at["x"] * 4 + (at["z"] % 2) * 2 + at["c"], "col": (at["z"] // 2) * 4 + at["y"]}
-
-
-def neighbour(at, axis, hops):
-    moved = dict(at)
-    moved[axis] = (at[axis] + hops) % 4
-    return device(moved)
-
-
-def sibling(at):
-    moved = dict(at)
-    moved["c"] = 1 - at["c"]
-    return device(moved)
 
 
 def block(gathered, strip, at, whole, half=None):
@@ -100,23 +90,19 @@
     ]
     for copy in small:
         copy.start()
-    loads = []
-    for p in range(PAIRS):
-        rows = pl.ds(p * ROWS, ROWS)
-        loads.append(pltpu.make_async_copy(lam_hbm.at[p], masked_ref.at[rows, :], load_sem.at[0, p]))
-        loads.append(pltpu.make_async_copy(const_hbm.at[p], const_ref.at[rows, :], load_sem.at[1, p]))
-    for copy in loads:
-        copy.start()
+    def load(p):
+        rows = pl.ds(pl.multiple_of(p * ROWS, ROWS), ROWS)
+        pltpu.make_async_copy(lam_hbm.at[p], masked_ref.at[rows, :], load_sem.at[0, p]).start()
+        pltpu.make_async_copy(const_hbm.at[p], const_ref.at[rows, :], load_sem.at[1, p]).start()
 
     def wait_blocks(ref, sem):
         pltpu.make_async_copy(ref, ref, sem).wait()
 
-    wait_blocks(gathered.at[:, 0, 0, 0, 0, 0], own_sem)
     pl.semaphore_wait(barrier, len(partners))
 
-    def send(part, target, stream, recv):
+    def send(part, target, stream, recv, source=None):
         pltpu.make_async_remote_copy(
-            src_ref=part,
+            src_ref=part if source is None else source,
             dst_ref=part,
             send_sem=send_sem.at[STREAMS.index(stream)],
             recv_sem=recv,
@@ -125,23 +111,24 @@
         ).start()
 
     def spread_one(s):
-        order = ORDERS[s % 3]
+        order = ORDERS[s]
         for hops in (2, 1, 3):
-            send(block(gathered, s, at, ""), moved(at, order[0], hops), "one", recv_one)
+            source = dress_hbm.at[:, pl.ds(s * WIDTH, WIDTH)]
+            send(block(gathered, s, at, ""), moved(at, order[0], hops), "one", recv_one, source)
 
     def spread_two(s):
-        order = ORDERS[s % 3]
+        order = ORDERS[s]
         for hops in (2, 1, 3):
             send(block(gathered, s, at, order[0]), moved(at, order[1], hops), "two", recv_two.at[s])
 
     def spread_ring(s):
-        order = ORDERS[s % 3]
+        order = ORDERS[s]
         for hops in (1, 3):
             send(block(gathered, s, at, order[:2]), moved(at, order[2], hops), "ring", recv_ring.at[s])
         send(block(gathered, s, at, order[:2]), other_core, "side", recv_side.at[0, s])
 
     def relay(s):
-        order = ORDERS[s % 3]
+        order = ORDERS[s]
         wait_blocks(gathered.at[s, 0:2, :, :, 0, :], recv_ring.at[s])
         for hops, half in ((1, 0), (3, 1)):
             source = moved(at, order[2], -hops)
@@ -150,7 +137,7 @@
             send(block(gathered, s, moved(at, order[2], hops), order[:2]), other_core, "side", recv_side.at[1, s])
 
     def land(s):
-        order = ORDERS[s % 3]
+        order = ORDERS[s]
         wait_blocks(gathered.at[s, 0, :, :, 0, :], recv_relay.at[s])
         send(block(gathered, s, moved(at, order[2], 2), order[:2]), other_core, "side", recv_side.at[2, s])
 
@@ -175,14 +162,20 @@
         rowmask[p] = jnp.sum(row_hot * mask[p : p + 1, :], axis=1, keepdims=True)
     squares[...] = jnp.zeros_like(squares)
 
+    wait_blocks(gathered.at[:, 0, 0, 0, 0, 0], own_sem)
     wait_blocks(gathered.at[:, 0:3, 0, 0, 0, 0], recv_one)
     for s in range(STRIPS):
         spread_two(s)
 
-    def prepare(p):
-        rows = pl.ds(p * ROWS, ROWS)
-        loads[2 * p].wait()
-        loads[2 * p + 1].wait()
+    def prepare(p, carry):
+        rows = pl.ds(pl.multiple_of(p * ROWS, ROWS), ROWS)
+        for ref, k in ((masked_ref, 0), (const_ref, 1)):
+            pltpu.make_async_copy(ref.at[rows, :], ref.at[rows, :], load_sem.at[k, p]).wait()
+
+        @pl.when(p + AHEAD < PAIRS)
+        def _():
+            load(p + AHEAD)
+
         for q in range(V // 256):
             cols = pl.ds(q * 256, 256)
             domain = (rowmask[p] * colmask[p, :, cols]).astype(BF16)
@@ -191,36 +184,19 @@
             pieces = [part[:, k * 64 : (k + 1) * 64] for k in (0, 2, 1, 3)]
             turned[rows, cols] = jnp.concatenate(pieces, axis=1)
             const_ref[rows, cols] = const_ref[rows, cols] * domain
+        return carry
 
     def arrive_two(s):
         wait_blocks(gathered.at[s, 0:3, 0, 0, 0, :], recv_two.at[s])
         spread_ring(s)
 
-    for p in (0, 1, 2):
-        prepare(p)
     for s in GROUPS[0]:
         arrive_two(s)
-    for p in (3, 4, 5):
-        prepare(p)
+    for p in range(AHEAD):
+        load(p)
     for s in GROUPS[1]:
         arrive_two(s)
-
-    def multiply(first, last):
-        def strip(s, carry):
-            cols = pl.ds(pl.multiple_of(s * WIDTH, WIDTH), WIDTH)
-            right = gathered[s].reshape(V, WIDTH)
-            product = jnp.dot(turned[...], right, preferred_element_type=F32)
-            total = jnp.zeros((8, WIDTH), F32)
-            for p in range(PAIRS):
-                rows = pl.ds(p * ROWS, ROWS)
-                part = const_ref[rows, cols].astype(F32) + colmask[p, :, cols] * product[p * ROWS : (p + 1) * ROWS, :]
-                resid_ref[rows, cols] = part
-                total = total + jnp.sum((part * part).reshape(ROWS // 8, 8, WIDTH), axis=0)
-            squares[...] += total
-            return carry
-
-        lax.fori_loop(first, last, strip, 0)
-
+    lax.fori_loop(0, PAIRS, prepare, 0)
     for s in GROUPS[0]:
         relay(s)
     for s in GROUPS[2]:
@@ -229,41 +205,60 @@
         relay(s)
     for s in GROUPS[0]:
         land(s)
-    for s in GROUPS[0]:
+
+    def strip(s, carry):
+        @pl.when(s == 1)
+        def _():
+            for later in GROUPS[2]:
+                relay(later)
+            for later in GROUPS[1]:
+                land(later)
+
+        @pl.when(s == 4)
+        def _():
+            for later in GROUPS[2]:
+                land(later)
+
         ready(s)
-    multiply(0, 2)
-    for s in GROUPS[2]:
-        relay(s)
-    for s in GROUPS[1]:
-        land(s)
-    multiply(2, 3)
-    for s in GROUPS[1]:
-        ready(s)
-    multiply(3, 5)
-    for s in GROUPS[2]:
-        land(s)
-    multiply(5, 6)
-    for s in GROUPS[2]:
-        ready(s)
-    multiply(6, 8)
+        cols = pl.ds(pl.multiple_of(s * WIDTH, WIDTH), WIDTH)
+
+        def rows_of(i, carry):
+            rows = pl.ds(pl.multiple_of(i * MTILE, MTILE), MTILE)
+            product = jnp.dot(turned[rows, :], gathered[s].reshape(V, WIDTH), preferred_element_type=F32)
+            total = jnp.zeros((8, WIDTH), F32)
+            for q in range(MTILE // ROWS):
+                p = i * (MTILE // ROWS) + q
+                pair_rows = pl.ds(pl.multiple_of(p * ROWS, ROWS), ROWS)
+                part = const_ref[pair_rows, cols].astype(F32) + colmask[p, :, cols] * product[q * ROWS : (q + 1) * ROWS, :]
+                resid_ref[pair_rows, cols] = part
+                total = total + jnp.sum((part * part).reshape(ROWS // 8, 8, WIDTH), axis=0)
+            squares[...] += total
+            return carry
+
+        lax.fori_loop(0, PAIRS * ROWS // MTILE, rows_of, 0)
+        return carry
+
+    lax.fori_loop(0, STRIPS, strip, 0)
 
     eight = squares[:, :128] + squares[:, 128:]
     mine[...] = jnp.sum(eight, axis=0, keepdims=True)
     me = lax.axis_index("row") * 8 + col
 
-    def tell(step, carry):
-        other = (me + step) % DEVICES
+    offsets = [(dx, dy, dz, dc) for dx in range(4) for dy in range(4) for dz in range(4) for dc in range(2)][1:]
+    offsets.sort(key=lambda o: (-sum(min(d, 4 - d) for d in o[:3]), o))
+    xs, ys, zs = ([(at[a] + d) % 4 for d in range(4)] for a in "xyz")
+    row_parts = [[x * 4 + (z % 2) * 2 for z in zs] for x in xs]
+    col_parts = [[(z // 2) * 4 + y for z in zs] for y in ys]
+    for dx, dy, dz, dc in offsets:
+        core = at["c"] if dc == 0 else other_core["c"]
         pltpu.make_async_remote_copy(
             src_ref=mine,
             dst_ref=everyone.at[me],
             send_sem=sum_send,
             recv_sem=sum_recv,
-            device_id={"row": other // 8, "col": other % 8},
+            device_id={"row": row_parts[dx][dz] + core, "col": col_parts[dy][dz]},
             device_id_type=MESH,
         ).start()
-        return carry
-
-    lax.fori_loop(1, DEVICES, tell, 0, unroll=True)
     everyone[me] = mine[...]
 
     own_energy = energy_ref[:, pl.ds(pl.multiple_of(col * ROWS, ROWS), ROWS)]

time: 56.7 us -> 54.7 us (0.965)
  Pallas kernels: 56.4 us -> 54.6 us
    pallas_call x1, Pallas kernels: 52.7 us -> 50.9 us  [per_device(): pl.pallas_call(gather_kernel, name='gather_multiply', out_shape=(pltpu.VM...]
where the time goes in v3:
time: 54.7 us; the launch traced here: 54.6 us
  Pallas kernels  54.6 us (100%)
    pallas_call x1, Pallas kernels, per_device(): pl.pallas_call(gather_kernel, name='gather_multiply', out_shape=(pltpu.VM...  50.9 us
    pallas_call x1, Pallas kernels, per_device(): pl.pallas_call(update_kernel, name='scale_update', out_shape=jax.ShapeDty...  3.66 us

profile of v3, /device:TPU:1, one launch (start us, length us, event | category | flops | bytes accessed | tf_op | source)
XLA Modules:
  0.0 54.6 jit_solution(17034171443059787638)
XLA Ops:
  0.0 50.9 %gather_multiply.1 = (f32[1536,2048]{1,0:T(8,128)S(1)}, bf16[1536,2048]{1,0:T(8,128)(2,1)S(1)}, f32[8,128]{1,0:T(8,128)S(1)}) custom-call(bf16[6,256,2048]{2,1,0:T(8,128)(2,1)} %lam_hbm.1, bf16[16,2048]{1,0:T(8,128)(2,1)} %dress_hbm.1, bf16[6,256,2048]{2,1,0:T(8,128)(2,1)} %const_hbm.1, s32[6,32]{1,0:T(8,128)} %mask_hbm.1, f32[1,2048]{1,0:T(1,128)} %bitcast.2, ...), custom_call_target="tpu_custom_call" | custom-call | tf_op jit(solution)/shard_map/gather_multiply/pallas_call | solution.py:309
  50.9 3.7 %scale_update.1 = bf16[1536,2048]{1,0:T(8,128)(2,1)} custom-call(f32[1536,2048]{1,0:T(8,128)S(1)} %get-tuple-element.8.resid_ref, bf16[1536,2048]{1,0:T(8,128)(2,1)S(1)} %get-tuple-element.9.masked_ref, f32[8,128]{1,0:T(8,128)S(1)} %get-tuple-element.10.factor_ref), custom_call_target="tpu_custom_call" | custom-call | tf_op jit(solution)/shard_map/scale_update/pallas_call | solution.py:345

commit v4 on v3

--- a/solution.py
+++ b/solution.py
@@ -197,17 +197,63 @@
     for s in GROUPS[1]:
         arrive_two(s)
     lax.fori_loop(0, PAIRS, prepare, 0)
+
+    def plane_product(s, axis, hops):
+        there = moved(at, axis, hops)
+        if axis == "x":
+            left = turned[:, pl.ds(pl.multiple_of(there["x"] * 512, 512), 512)]
+            right = gathered[s, there["x"]]
+        else:
+            offset = there["zl"] * 256 + there["zh"] * 128
+            pieces = [turned[:, pl.ds(pl.multiple_of(x * 512 + offset, 128), 128)] for x in range(4)]
+            left = jnp.concatenate(pieces, axis=1)
+            right = gathered[s, :, there["zl"], there["zh"]]
+        return jnp.dot(left, right.reshape(512, WIDTH), preferred_element_type=F32)
+
+    def near(s, axis):
+        cols = pl.ds(s * WIDTH, WIDTH)
+        wait_blocks(gathered.at[s, 0, :, :, 0, :], recv_side.at[0, s])
+        resid_ref[:, cols] = const_ref[:, cols].astype(F32) + plane_product(s, axis, 0)
+
+    def beside(s, axis):
+        cols = pl.ds(s * WIDTH, WIDTH)
+        wait_blocks(gathered.at[s, 0:2, :, :, 0, :], recv_side.at[1, s])
+
+        def add(k, carry):
+            resid_ref[:, cols] += plane_product(s, axis, 2 * k + 1)
+            return carry
+
+        lax.fori_loop(0, 2, add, 0)
+
+    def far(s, axis):
+        cols = pl.ds(s * WIDTH, WIDTH)
+        wait_blocks(gathered.at[s, 0, :, :, 0, :], recv_side.at[2, s])
+        product = plane_product(s, axis, 2)
+        total = jnp.zeros((8, WIDTH), F32)
+        for p in range(PAIRS):
+            rows = pl.ds(p * ROWS, ROWS)
+            part = colmask[p, :, cols] * (resid_ref[rows, cols] + product[p * ROWS : (p + 1) * ROWS, :])
+            resid_ref[rows, cols] = part
+            total = total + jnp.sum((part * part).reshape(ROWS // 8, 8, WIDTH), axis=0)
+        squares[...] += total
+
     for s in GROUPS[0]:
         relay(s)
     for s in GROUPS[2]:
         arrive_two(s)
+    near(0, "x")
+    near(1, "z")
     for s in GROUPS[1]:
         relay(s)
+    beside(0, "x")
+    beside(1, "z")
     for s in GROUPS[0]:
         land(s)
+    far(0, "x")
+    far(1, "z")
 
     def strip(s, carry):
-        @pl.when(s == 1)
+        @pl.when(s == 2)
         def _():
             for later in GROUPS[2]:
                 relay(later)
@@ -238,7 +284,7 @@
         lax.fori_loop(0, PAIRS * ROWS // MTILE, rows_of, 0)
         return carry
 
-    lax.fori_loop(0, STRIPS, strip, 0)
+    lax.fori_loop(2, STRIPS, strip, 0)
 
     eight = squares[:, :128] + squares[:, 128:]
     mine[...] = jnp.sum(eight, axis=0, keepdims=True)
@@ -287,7 +333,7 @@
     wait_blocks(everyone.at[0 : DEVICES - 1], sum_send)
 
 
-CHUNK = 128
+CHUNK = 64
 
 
 def update_kernel(resid_ref, masked_ref, factor_ref, out_hbm, staged, sem):

time: 54.7 us -> 53.7 us (0.982)
  Pallas kernels: 54.6 us -> 53.6 us
    pallas_call x1, Pallas kernels: 50.9 us -> 50.1 us  [per_device(): pl.pallas_call(gather_kernel, name='gather_multiply', out_shape=(pltpu.VM...]
where the time goes in v4:
time: 53.7 us; the launch traced here: 53.6 us
  Pallas kernels  53.6 us (100%)
    pallas_call x1, Pallas kernels, per_device(): pl.pallas_call(gather_kernel, name='gather_multiply', out_shape=(pltpu.VM...  50.1 us
    pallas_call x1, Pallas kernels, per_device(): pl.pallas_call(update_kernel, name='scale_update', out_shape=jax.ShapeDty...  3.5 us

profile of v4, /device:TPU:1, one launch (start us, length us, event | category | flops | bytes accessed | tf_op | source)
XLA Modules:
  0.0 53.6 jit_solution(4444777498722278638)
XLA Ops:
  0.0 50.1 %gather_multiply.1 = (f32[1536,2048]{1,0:T(8,128)S(1)}, bf16[1536,2048]{1,0:T(8,128)(2,1)S(1)}, f32[8,128]{1,0:T(8,128)S(1)}) custom-call(bf16[6,256,2048]{2,1,0:T(8,128)(2,1)} %lam_hbm.1, bf16[16,2048]{1,0:T(8,128)(2,1)} %dress_hbm.1, bf16[6,256,2048]{2,1,0:T(8,128)(2,1)} %const_hbm.1, s32[6,32]{1,0:T(8,128)} %mask_hbm.1, f32[1,2048]{1,0:T(1,128)} %bitcast.2, ...), custom_call_target="tpu_custom_call" | custom-call | tf_op jit(solution)/shard_map/gather_multiply/pallas_call | solution.py:355
  50.1 3.5 %scale_update.1 = bf16[1536,2048]{1,0:T(8,128)(2,1)} custom-call(f32[1536,2048]{1,0:T(8,128)S(1)} %get-tuple-element.8.resid_ref, bf16[1536,2048]{1,0:T(8,128)(2,1)S(1)} %get-tuple-element.9.masked_ref, f32[8,128]{1,0:T(8,128)S(1)} %get-tuple-element.10.factor_ref), custom_call_target="tpu_custom_call" | custom-call | tf_op jit(solution)/shard_map/scale_update/pallas_call | solution.py:391

commit v5 on v4

--- a/solution.py
+++ b/solution.py
@@ -65,8 +65,8 @@
 
 def gather_kernel(
     lam_hbm, dress_hbm, const_hbm, mask_hbm, energy_hbm, shift_hbm,
-    resid_ref, masked_ref, factor_ref,
-    gathered, turned, const_ref, mask_ref, energy_ref, shift_ref, colmask, rowmask, squares, mine, everyone,
+    resid_ref, wide_ref, factor_ref,
+    masked_ref, gathered, turned, const_ref, mask_ref, energy_ref, shift_ref, colmask, rowmask, squares, mine, everyone,
     small_sem, load_sem, own_sem, send_sem, recv_one, recv_two, recv_ring, recv_relay, recv_side, sum_send, sum_recv,
 ):
     at = place()
@@ -320,6 +320,13 @@
 
     lax.fori_loop(0, PAIRS, divide, 0)
 
+    def widen(p, carry):
+        rows = pl.ds(pl.multiple_of(p * ROWS, ROWS), ROWS)
+        wide_ref[rows, :] = masked_ref[rows, :].astype(F32)
+        return carry
+
+    lax.fori_loop(0, PAIRS, widen, 0)
+
     wait_blocks(everyone.at[0 : DEVICES - 1], sum_recv)
     total = jnp.sum(jnp.sum(everyone[...], axis=0), axis=1, keepdims=True)
     factor = 0.25 * lax.rsqrt(total / ENTRIES + 1e-06)
@@ -341,7 +348,7 @@
     copies = []
     for i in range(PAIRS * ROWS // CHUNK):
         rows = pl.ds(i * CHUNK, CHUNK)
-        staged[rows, :] = (masked_ref[rows, :].astype(F32) + factor * resid_ref[rows, :]).astype(BF16)
+        staged[rows, :] = (masked_ref[rows, :] + factor * resid_ref[rows, :]).astype(BF16)
         copies.append(pltpu.make_async_copy(staged.at[rows, :], out_hbm.at[rows, :], sem.at[i]))
         copies[-1].start()
     for copy in copies:
@@ -355,10 +362,11 @@
     resid, masked, factor = pl.pallas_call(
         gather_kernel,
         name="gather_multiply",
-        out_shape=(pltpu.VMEM(flat, F32), pltpu.VMEM(flat, BF16), pltpu.VMEM((8, 128), F32)),
+        out_shape=(pltpu.VMEM(flat, F32), pltpu.VMEM(flat, F32), pltpu.VMEM((8, 128), F32)),
         in_specs=[hbm] * 6,
         out_specs=(vmem, vmem, vmem),
         scratch_shapes=[
+            pltpu.VMEM(flat, BF16),
             pltpu.VMEM((STRIPS, 4, 2, 2, 2, 4, 16, WIDTH), BF16),
             pltpu.VMEM(flat, BF16),
             pltpu.VMEM(flat, BF16),
@@ -395,7 +403,7 @@
         in_specs=[vmem, vmem, vmem],
         out_specs=hbm,
         scratch_shapes=[pltpu.VMEM(flat, BF16), dma((PAIRS * ROWS // CHUNK,))],
-        compiler_params=pltpu.CompilerParams(vmem_limit_bytes=16 << 20),
+        compiler_params=pltpu.CompilerParams(vmem_limit_bytes=8 << 20),
     )(resid, masked, factor)
     return out.reshape(PAIRS, ROWS, V)
 

time: 53.7 us -> 53.2 us (level)
  no operation moved by 1% of the time
where the time goes in v5:
time: 53.2 us; the launch traced here: 53.1 us
  Pallas kernels  53.1 us (100%)
    pallas_call x1, Pallas kernels, per_device(): pl.pallas_call(gather_kernel, name='gather_multiply', out_shape=(pltpu.VM...  50.1 us
    pallas_call x1, Pallas kernels, per_device(): pl.pallas_call(update_kernel, name='scale_update', out_shape=jax.ShapeDty...  3.01 us

profile of v5, /device:TPU:1, one launch (start us, length us, event | category | flops | bytes accessed | tf_op | source)
XLA Modules:
  0.0 53.1 jit_solution(9168600106968630636)
XLA Ops:
  0.0 50.1 %gather_multiply.1 = (f32[1536,2048]{1,0:T(8,128)S(1)}, f32[1536,2048]{1,0:T(8,128)S(1)}, f32[8,128]{1,0:T(8,128)S(1)}) custom-call(bf16[6,256,2048]{2,1,0:T(8,128)(2,1)} %lam_hbm.1, bf16[16,2048]{1,0:T(8,128)(2,1)} %dress_hbm.1, bf16[6,256,2048]{2,1,0:T(8,128)(2,1)} %const_hbm.1, s32[6,32]{1,0:T(8,128)} %mask_hbm.1, f32[1,2048]{1,0:T(1,128)} %bitcast.2, ...), custom_call_target="tpu_custom_call" | custom-call | tf_op jit(solution)/shard_map/gather_multiply/pallas_call | solution.py:362
  50.1 3.0 %scale_update.1 = bf16[1536,2048]{1,0:T(8,128)(2,1)} custom-call(f32[1536,2048]{1,0:T(8,128)S(1)} %get-tuple-element.8.resid_ref, f32[1536,2048]{1,0:T(8,128)S(1)} %get-tuple-element.9.masked_ref, f32[8,128]{1,0:T(8,128)S(1)} %get-tuple-element.10.factor_ref), custom_call_target="tpu_custom_call" | custom-call | tf_op jit(solution)/shard_map/scale_update/pallas_call | solution.py:399
